TPU v7x, 512 devices: a whole 4x4x16 slice. The times are simulated.
512 devices in a mesh: grp: 8 (over y, core), dev: 64 (over z, x).
Axes of the slice: x: 4, y: 4, z: 16, core: 2. Of those that a mesh axis runs over, the one named last changes fastest.
Arguments:
- right_side: float32 [512, 8192], P('grp', 'dev'), may hold values from -6 to 6
- previous: float32 [512, 8192], P('grp', 'dev'), may hold values from -4 to 4
- east_face: float32 [512, 8192], P('grp', 'dev'), may hold values from 0.5 to 10
- south_face: float32 [512, 8192], P('grp', 'dev'), may hold values from 0.5 to 10
- wet_mask: int32 [512, 8192], P('grp', 'dev'), may hold values from 0 to 1, as said below
Outputs:
- surface: float32 [512, 8192], P('grp', 'dev')
- residual: float32 [512, 8192], P('grp', 'dev')
Inputs may be any that keep to these rules, and one draw needn't show every extreme that they name: `wet_mask`: dry cells form axis-aligned rectangles of 1 to 7 by 1 to 7 cells; each lies inside one aligned tile of 16 x 16 cells, one cell or more away from the tile's border, at most one rectangle a tile.
All inputs are finite; a program needn't handle non-finite values.
Results may differ from a plain program's by a relative error of at most 0.0003.
Values sent between devices are 32-bit elements; how exact they have to be, the bound alone decides.
No kernel may reach another device: no remote copies, remote signals or barrier semaphores. Data moves between devices by JAX's collectives and lax.ppermute only.
A program may use at most 64 MiB of HBM per device.

v0:
```python
import jax
import jax.numpy as jnp
from jax import lax
from jax.sharding import PartitionSpec as P

CYCLES = 2
PRE = 2
POST = 2
COARSE_SWEEPS = 4
relax_weight = 0.8
wet_mass = 2e-05


def extended_2(value, sides, width):
    for axis, dim in sides:
        peers, length = (lax.axis_size(axis), value.shape[dim])
        up = [(i, (i + 1) % peers) for i in range(peers - 1)]
        down = [(j, i) for i, j in up]
        last = lax.slice_in_dim(value, length - width, length, axis=dim)
        initial = lax.slice_in_dim(value, 0, width, axis=dim)
        before = lax.ppermute(last, axis, up)
        after = lax.ppermute(initial, axis, down)
        value = jnp.concatenate([before, value, after], axis=dim)
    return value


def coarsen_sum(values):
    row_count, col_count = values.shape
    return values.reshape(row_count // 2, 2, col_count // 2, 2).sum(axis=(1, 3))


def coarsen_links(coefficients):
    mass_term, east_link, west_link, south_link, north_link = coefficients
    return (
        coarsen_sum(mass_term),
        east_link[0::2, 1::2] + east_link[1::2, 1::2],
        west_link[0::2, 0::2] + west_link[1::2, 0::2],
        south_link[1::2, 0::2] + south_link[1::2, 1::2],
        north_link[0::2, 0::2] + north_link[0::2, 1::2],
    )


def inverse_diagonal(coefficients):
    mass_term, east_link, west_link, south_link, north_link = coefficients
    return 1.0 / (mass_term + east_link + west_link + south_link + north_link)


def operate(padded, coefficients):
    mass_term, east_link, west_link, south_link, north_link = coefficients
    centre = padded[1:-1, 1:-1]
    return (
        mass_term * centre
        + east_link * (centre - padded[1:-1, 2:])
        + west_link * (centre - padded[1:-1, :-2])
        + south_link * (centre - padded[2:, 1:-1])
        + north_link * (centre - padded[:-2, 1:-1])
    )


def jacobi_sweep(values, padded, source, coefficients, inverse):
    return values + relax_weight * (source - operate(padded, coefficients)) * inverse


def zero_padded(values):
    return jnp.pad(values, 1)


def block_padded(values):
    return extended_2(values, (("grp", 0), ("dev", 1)), 1)


def strip_padded(values):
    row_padded = extended_2(values, (("grp", 0),), 1)
    return jnp.pad(row_padded, ((0, 0), (1, 1)))


def prolong(values):
    return jnp.repeat(jnp.repeat(values, 2, axis=0), 2, axis=1)


def smoothing(values, source, coefficients, inverse, sweeps, from_zero, padder):
    for sweep_index in range(sweeps):
        if from_zero and sweep_index == 0:
            values = relax_weight * source * inverse
        else:
            values = jacobi_sweep(values, padder(values), source, coefficients, inverse)
    return values


def unstack(stacked):
    return tuple((stacked[position] for position in range(5)))


def shards(right_side, previous, east_face, south_face, wet_mask):
    group_index = lax.axis_index("grp")
    member_index = lax.axis_index("dev")
    wet = wet_mask.astype(jnp.float32)
    extended = extended_2(jnp.stack([wet, east_face, south_face]), (("grp", 1), ("dev", 2)), 1)
    wet_pad = extended[0]
    east_pad = extended[1]
    south_pad = extended[2]
    east_link = east_face * wet * wet_pad[1:-1, 2:]
    west_link = east_pad[1:-1, :-2] * wet_pad[1:-1, :-2] * wet
    south_link = south_face * wet * wet_pad[2:, 1:-1]
    north_link = south_pad[:-2, 1:-1] * wet_pad[:-2, 1:-1] * wet
    mass_term = wet * wet_mass + (1.0 - wet)
    source = wet * right_side + (1.0 - wet) * previous
    hierarchy = [(mass_term, east_link, west_link, south_link, north_link)]
    for level_index in range(3):
        hierarchy.append(coarsen_links(hierarchy[-1]))
    inverses = [inverse_diagonal(coefficients) for coefficients in hierarchy]
    strip_coefficients = unstack(lax.all_gather(jnp.stack(hierarchy[3]), "dev", axis=2, tiled=True))
    strip_inverse = inverse_diagonal(strip_coefficients)
    coarse_coefficients = coarsen_links(strip_coefficients)
    whole_coefficients = unstack(
        lax.all_gather(jnp.stack(coarse_coefficients), "grp", axis=1, tiled=True)
    )
    whole_inverse = inverse_diagonal(whole_coefficients)
    whole_mass = jnp.sum(whole_coefficients[0])

    def coarse_level(local_source):
        strip_source = lax.all_gather(local_source, "dev", axis=1, tiled=True)
        strip_values = smoothing(
            None, strip_source, strip_coefficients, strip_inverse, PRE, True, strip_padded
        )
        strip_rest = coarsen_sum(
            strip_source - operate(strip_padded(strip_values), strip_coefficients)
        )
        strip_rows = strip_rest.shape[0]
        whole_source = lax.all_gather(strip_rest, "grp", axis=0, tiled=True)
        whole_values = smoothing(
            None, whole_source, whole_coefficients, whole_inverse, COARSE_SWEEPS, True, zero_padded
        )
        whole_rest = whole_source - operate(zero_padded(whole_values), whole_coefficients)
        shift_value = relax_weight * jnp.sum(whole_rest) / whole_mass
        coarse_values = lax.dynamic_slice_in_dim(
            whole_values, group_index * strip_rows, strip_rows, 0
        )
        coarse_values = coarse_values + shift_value
        strip_values = strip_values + prolong(coarse_values)
        strip_values = smoothing(
            strip_values, strip_source, strip_coefficients, strip_inverse, POST, False, strip_padded
        )
        local_width = local_source.shape[1]
        return lax.dynamic_slice_in_dim(strip_values, member_index * local_width, local_width, 1)

    def descend(level_index, values, level_source, from_zero):
        if level_index == 3:
            return coarse_level(level_source)
        coefficients = hierarchy[level_index]
        values = smoothing(
            values, level_source, coefficients, inverses[level_index], PRE, from_zero, block_padded
        )
        remainder = coarsen_sum(level_source - operate(block_padded(values), coefficients))
        values = values + prolong(descend(level_index + 1, None, remainder, True))
        return smoothing(
            values, level_source, coefficients, inverses[level_index], POST, False, block_padded
        )

    surface = previous
    for cycle_index in range(CYCLES):
        surface = descend(0, surface, source, False)
    residual = source - operate(block_padded(surface), hierarchy[0])
    return (surface, residual)


def solution(mesh):
    placed = (P("grp", "dev"), P("grp", "dev"), P("grp", "dev"), P("grp", "dev"), P("grp", "dev"))
    return jax.shard_map(
        shards,
        mesh=mesh,
        in_specs=placed,
        out_specs=(P("grp", "dev"), P("grp", "dev")),
        check_vma=False,
    )
```

profile of v0, /device:TPU:129, one launch (start us, length us, event | category | flops | bytes accessed | tf_op | source)
XLA Modules:
  0.0 903.5 jit_solution(13340431999990689571)
XLA Ops:
  21.1 5.5 collective-permute-start.3
  78.6 4.8 collective-permute-start.16
  117.8 81.8 %all_gather.19 = f32[5,8,1024]{1,0,2:T(8,128)S(1)} all-gather(f32[5,8,16]{1,0,2:T(8,128)S(1)} %copy.45), channel_id=1, replica_groups=mesh['grp'=8,'dev'=64] {'dev'}, dimensions={2}, use_global_device_ids=true | all-gather | bytes 166400 | tf_op jit(solution)/shard_map/all_gather | solution.py:112
  208.2 25.2 %collective-permute-start.24 = (f32[1,32]{1,0:T(1,128)S(1)}, f32[1,32]{1,0:T(1,128)S(1)}, u32[]{:S(2)}, u32[]{:S(2)}) collective-permute-start(f32[1,32]{1,0:T(1,128)S(1)} %get-tuple-element.169), channel_id=1, source_target_pairs={{0,64},{64,128},{128,192},{192,256},{256,320},{320,384},{384,448},... | collective-permute-start | bytes 392 | tf_op jit(solution)/shard_map/ppermute | solution.py:21
  244.6 5.8 collective-permute-done.27
  264.2 4.4 collective-permute-done.31
  268.9 59.9 %all-gather = f32[64,16,8]{1,2,0:T(8,128)S(1)} all-gather(f32[1,16,8]{1,2,0:T(8,128)S(1)} %bitcast.353), channel_id=1, replica_groups=mesh['grp'=8,'dev'=64] {'dev'}, dimensions={0}, use_global_device_ids=true | all-gather | bytes 33280 | tf_op jit(solution)/shard_map/all_gather | solution.py:122
  329.1 21.8 %collective-permute-start.32 = (f32[1,1024]{1,0:T(1,128)S(1)}, f32[1,1024]{1,0:T(1,128)S(1)}, u32[]{:S(2)}, u32[]{:S(2)}) collective-permute-start(f32[1,1024]{1,0:T(1,128)S(1)} %get-tuple-element.97), channel_id=1, source_target_pairs={{0,64},{64,128},{128,192},{192,256},{256,320},{320,384},{384,448},... | collective-permute-start | bytes 12296 | tf_op jit(solution)/shard_map/ppermute | solution.py:21
  352.8 14.5 %all_gather.21 = f32[5,32,512]{2,0,1:T(8,128)S(1)} all-gather(f32[5,4,512]{2,0,1:T(8,128)S(1)} %copy.51), channel_id=1, replica_groups=mesh['grp'=8,'dev'=64] {'grp'}, dimensions={1}, use_global_device_ids=true | all-gather | bytes 368640 | tf_op jit(solution)/shard_map/all_gather | solution.py:116
  377.4 11.2 %all-gather.1 = f32[8,4,512]{2,1,0:T(4,128)S(1)} all-gather(f32[1,4,512]{2,1,0:T(4,128)S(1)} %bitcast.350), channel_id=1, replica_groups=mesh['grp'=8,'dev'=64] {'grp'}, dimensions={0}, use_global_device_ids=true | all-gather | bytes 73728 | tf_op jit(solution)/shard_map/all_gather | solution.py:130
  420.8 5.8 collective-permute-done.43
  458.6 4.5 collective-permute-done.51
  476.7 4.5 collective-permute-done.55
  494.9 4.6 collective-permute-done.59
  513.3 4.6 collective-permute-done.63
  531.4 4.6 collective-permute-done.67
  549.6 4.6 collective-permute-done.71
  567.7 4.6 collective-permute-done.75
  588.4 4.5 collective-permute-done.79
  606.3 4.5 collective-permute-done.83
  625.0 4.4 collective-permute-done.87
  642.9 4.4 collective-permute-done.91
  647.6 60.0 %all-gather.2 = f32[64,16,8]{1,2,0:T(8,128)S(1)} all-gather(f32[1,16,8]{1,2,0:T(8,128)S(1)} %bitcast.354), channel_id=1, replica_groups=mesh['grp'=8,'dev'=64] {'dev'}, dimensions={0}, use_global_device_ids=true | all-gather | bytes 33280 | tf_op jit(solution)/shard_map/all_gather | solution.py:122
  707.8 21.8 %collective-permute-start.92 = (f32[1,1024]{1,0:T(1,128)S(1)}, f32[1,1024]{1,0:T(1,128)S(1)}, u32[]{:S(2)}, u32[]{:S(2)}) collective-permute-start(f32[1,1024]{1,0:T(1,128)S(1)} %get-tuple-element.76), channel_id=1, source_target_pairs={{0,64},{64,128},{128,192},{192,256},{256,320},{320,384},{384,448},... | collective-permute-start | bytes 12296 | tf_op jit(solution)/shard_map/ppermute | solution.py:21
  744.3 11.2 %all-gather.3 = f32[8,4,512]{2,1,0:T(4,128)S(1)} all-gather(f32[1,4,512]{2,1,0:T(4,128)S(1)} %bitcast.349), channel_id=1, replica_groups=mesh['grp'=8,'dev'=64] {'grp'}, dimensions={0}, use_global_device_ids=true | all-gather | bytes 73728 | tf_op jit(solution)/shard_map/all_gather | solution.py:130
  787.4 5.8 collective-permute-done.103
  807.0 4.4 collective-permute-done.107
  825.1 4.5 collective-permute-done.111
  843.3 4.5 collective-permute-done.115
  861.5 4.6 collective-permute-done.119
  879.8 4.6 collective-permute-done.123
  898.0 4.6 collective-permute-done.127
  (535 shorter events, 480.6 us)
Async XLA Ops:
  1.4 12.8 %collective-permute-start.4 = (f32[1,128]{1,0:T(1,128)S(1)}, f32[1,128]{1,0:T(1,128)S(1)}, u32[]{:S(2)}, u32[]{:S(2)}) collective-permute-start(f32[1,128]{1,0:T(1,128)S(1)} %get-tuple-element.105), channel_id=1, source_target_pairs={{0,64},{64,128},{128,192},{192,256},{256,320},{320,384},{384,448},... | collective-permute-start | bytes 1544 | tf_op jit(solution)/shard_map/ppermute | solution.py:21
  5.1 9.0 collective-permute-start.5
  18.0 14.0 %collective-permute-start.2 = (f32[3,66,1]{2,1,0:T(8,128)S(1)}, f32[3,66,1]{2,1,0:T(8,128)S(1)}, u32[]{:S(2)}, u32[]{:S(2)}) collective-permute-start(f32[3,66,1]{2,1,0:T(8,128)S(1)} %get-tuple-element.34), channel_id=1, source_target_pairs={{0,1},{1,2},{2,3},{3,4},{4,5},{5,6},{6,7},{7,8},{8,9},{9,10},{10,1... | collective-permute-start | bytes 2384 | tf_op jit(solution)/shard_map/ppermute | solution.py:21
  21.1 10.9 %collective-permute-start.3 = (f32[3,66,1]{2,1,0:T(8,128)S(1)}, f32[3,66,1]{2,1,0:T(8,128)S(1)}, u32[]{:S(2)}, u32[]{:S(2)}) collective-permute-start(f32[3,66,1]{2,1,0:T(8,128)S(1)} %get-tuple-element.35), channel_id=1, source_target_pairs={{1,0},{2,1},{3,2},{4,3},{5,4},{6,5},{7,6},{8,7},{9,8},{10,9},{11,1... | collective-permute-start | bytes 2384 | tf_op jit(solution)/shard_map/ppermute | solution.py:22
  28.6 8.0 collective-permute-start.7
  48.5 8.0 collective-permute-start.11
  56.7 9.3 %collective-permute-start.12 = (f32[1,128]{1,0:T(1,128)S(1)}, f32[1,128]{1,0:T(1,128)S(1)}, u32[]{:S(2)}, u32[]{:S(2)}) collective-permute-start(f32[1,128]{1,0:T(1,128)S(1)} %get-tuple-element.101), channel_id=1, source_target_pairs={{0,64},{64,128},{128,192},{192,256},{256,320},{320,384},{384,448},... | collective-permute-start | bytes 1544 | tf_op jit(solution)/shard_map/ppermute | solution.py:21
  68.0 8.0 collective-permute-start.15
  90.3 7.8 collective-permute-start.19
  108.2 7.8 collective-permute-start.23
  208.2 27.2 %collective-permute-start.24 = (f32[1,32]{1,0:T(1,128)S(1)}, f32[1,32]{1,0:T(1,128)S(1)}, u32[]{:S(2)}, u32[]{:S(2)}) collective-permute-start(f32[1,32]{1,0:T(1,128)S(1)} %get-tuple-element.169), channel_id=1, source_target_pairs={{0,64},{64,128},{128,192},{192,256},{256,320},{320,384},{384,448},... | collective-permute-start | bytes 392 | tf_op jit(solution)/shard_map/ppermute | solution.py:21
  242.7 7.8 collective-permute-start.27
  260.8 7.8 collective-permute-start.31
  329.1 38.3 %collective-permute-start.32 = (f32[1,1024]{1,0:T(1,128)S(1)}, f32[1,1024]{1,0:T(1,128)S(1)}, u32[]{:S(2)}, u32[]{:S(2)}) collective-permute-start(f32[1,1024]{1,0:T(1,128)S(1)} %get-tuple-element.97), channel_id=1, source_target_pairs={{0,64},{64,128},{128,192},{192,256},{256,320},{320,384},{384,448},... | collective-permute-start | bytes 12296 | tf_op jit(solution)/shard_map/ppermute | solution.py:21
  350.9 16.4 %collective-permute-start.33 = (f32[1,1024]{1,0:T(1,128)S(1)}, f32[1,1024]{1,0:T(1,128)S(1)}, u32[]{:S(2)}, u32[]{:S(2)}) collective-permute-start(f32[1,1024]{1,0:T(1,128)S(1)} %get-tuple-element.96), channel_id=1, source_target_pairs={{64,0},{128,64},{192,128},{256,192},{320,256},{384,320},{448,384},... | collective-permute-start | bytes 12296 | tf_op jit(solution)/shard_map/ppermute | solution.py:22
  418.9 7.8 collective-permute-start.43
  455.2 7.8 collective-permute-start.51
  473.3 7.8 collective-permute-start.55
  491.5 8.0 collective-permute-start.59
  509.9 8.0 collective-permute-start.63
  528.0 8.0 collective-permute-start.67
  546.2 8.0 collective-permute-start.71
  564.4 8.0 collective-permute-start.75
  585.0 7.8 collective-permute-start.79
  603.0 7.8 collective-permute-start.83
  621.6 7.8 collective-permute-start.87
  707.8 23.7 %collective-permute-start.92 = (f32[1,1024]{1,0:T(1,128)S(1)}, f32[1,1024]{1,0:T(1,128)S(1)}, u32[]{:S(2)}, u32[]{:S(2)}) collective-permute-start(f32[1,1024]{1,0:T(1,128)S(1)} %get-tuple-element.76), channel_id=1, source_target_pairs={{0,64},{64,128},{128,192},{192,256},{256,320},{320,384},{384,448},... | collective-permute-start | bytes 12296 | tf_op jit(solution)/shard_map/ppermute | solution.py:21
  821.8 7.8 collective-permute-start.111
  839.9 7.8 collective-permute-start.115
  858.1 8.0 collective-permute-start.119
  876.4 8.0 collective-permute-start.123
  894.6 8.0 collective-permute-start.127
  (108 other events, 1214.5 us)
where the time goes:
time: 914 us; the launch traced here: 904 us
  starting transfers between devices  397 us (43%)
  blocking collectives  239 us (26%)
  waiting for transfers between devices  214 us (23%)
  local copies, waits for them, and re-layouts  30.7 us (3%)
  other arithmetic  16.4 us (2%)
    ppermute x64, starting transfers between devices, extended_2(): before = lax.ppermute(last, axis, up)  261 us
    ppermute x64, starting transfers between devices, extended_2(): after = lax.ppermute(initial, axis, down)  136 us
    ppermute x64, waiting for transfers between devices, extended_2(): before = lax.ppermute(last, axis, up)  123 us
    all_gather x2, blocking collectives, coarse_level(): strip_source = lax.all_gather(local_source, 'dev', axis=1, tiled=True)  120 us
    ppermute x64, waiting for transfers between devices, extended_2(): after = lax.ppermute(initial, axis, down)  91.4 us
    all_gather x1, blocking collectives, shards(): lax.all_gather(jnp.stack(hierarchy[3]), 'dev', axis=2, tiled=True)  81.8 us
    all_gather x2, blocking collectives, coarse_level(): whole_source = lax.all_gather(strip_rest, 'grp', axis=0, tiled=True)  22.4 us
  transfers between devices with their start and end apart: 128, of which 60 were waited for; matrix products, arithmetic and copies ran while one was open for 1% of the time, Pallas kernels for 0%

commit v1 on v0

--- a/solution.py
+++ b/solution.py
@@ -119,7 +119,9 @@
     whole_mass = jnp.sum(whole_coefficients[0])
 
     def coarse_level(local_source):
-        strip_source = lax.all_gather(local_source, "dev", axis=1, tiled=True)
+        strip_source = jnp.concatenate(
+            lax.all_to_all(jnp.stack([local_source] * lax.axis_size("dev")), "dev", 0, 0), axis=1
+        )
         strip_values = smoothing(
             None, strip_source, strip_coefficients, strip_inverse, PRE, True, strip_padded
         )

time: 914 us -> 801 us (0.88)
  blocking collectives: 239 us -> 135 us
  starting transfers between devices: 397 us -> 375 us
  waiting for transfers between devices: 214 us -> 224 us
    all_gather x2 -> x0, blocking collectives: 120 us -> none  [coarse_level(): strip_source = lax.all_gather(local_source, 'dev', axis=1, tiled=True)]
    ppermute x64, starting transfers between devices: 261 us -> 226 us  [extended_2(): before = lax.ppermute(last, axis, up)]
    all_to_all x0 -> x1, blocking collectives: none -> 16.2 us  [coarse_level(): lax.all_to_all(jnp.stack([local_source] * lax.axis_size('dev')), 'dev', 0...]
    all_to_all x0 -> x1, starting transfers between devices: none -> 11.3 us  [coarse_level(): lax.all_to_all(jnp.stack([local_source] * lax.axis_size('dev')), 'dev', 0...]
  transfers between devices with their start and end apart: 128 -> 129, of which waited for: 60 -> 61; matrix products, arithmetic and copies ran while one was open for 1% -> 2% of each run, Pallas kernels for 0% -> 0%
where the time goes in v1:
time: 801 us; the launch traced here: 790 us
  starting transfers between devices  375 us (47%)
  waiting for transfers between devices  224 us (28%)
  blocking collectives  135 us (17%)
  local copies, waits for them, and re-layouts  32.4 us (4%)
  other arithmetic  17.7 us (2%)
    ppermute x64, starting transfers between devices, extended_2(): before = lax.ppermute(last, axis, up)  226 us
    ppermute x64, starting transfers between devices, extended_2(): after = lax.ppermute(initial, axis, down)  137 us
    ppermute x64, waiting for transfers between devices, extended_2(): before = lax.ppermute(last, axis, up)  123 us
    ppermute x64, waiting for transfers between devices, extended_2(): after = lax.ppermute(initial, axis, down)  91.4 us
    all_gather x1, blocking collectives, shards(): lax.all_gather(jnp.stack(hierarchy[3]), 'dev', axis=2, tiled=True)  82 us
    all_gather x2, blocking collectives, coarse_level(): whole_source = lax.all_gather(strip_rest, 'grp', axis=0, tiled=True)  22.5 us
    all_to_all x1, blocking collectives, coarse_level(): lax.all_to_all(jnp.stack([local_source] * lax.axis_size('dev')), 'dev', 0...  16.2 us
  transfers between devices with their start and end apart: 129, of which 61 were waited for; matrix products, arithmetic and copies ran while one was open for 2% of the time, Pallas kernels for 0%

profile of v1, /device:TPU:129, one launch (start us, length us, event | category | flops | bytes accessed | tf_op | source)
XLA Modules:
  0.0 789.5 jit_solution(5940830660263661517)
XLA Ops:
  21.1 5.5 collective-permute-start.3
  78.6 4.8 collective-permute-start.16
  117.8 82.0 %all_gather.12 = f32[5,8,1024]{1,0,2:T(8,128)S(1)} all-gather(f32[5,8,16]{1,0,2:T(8,128)S(1)} %copy.40), channel_id=1, replica_groups=mesh['grp'=8,'dev'=64] {'dev'}, dimensions={2}, use_global_device_ids=true | all-gather | bytes 166400 | tf_op jit(solution)/shard_map/all_gather | solution.py:112
  207.7 25.2 %collective-permute-start.24 = (f32[1,32]{1,0:T(1,128)S(1)}, f32[1,32]{1,0:T(1,128)S(1)}, u32[]{:S(2)}, u32[]{:S(2)}) collective-permute-start(f32[1,32]{1,0:T(1,128)S(1)} %get-tuple-element.169), channel_id=1, source_target_pairs={{0,64},{64,128},{128,192},{192,256},{256,320},{320,384},{384,448},... | collective-permute-start | bytes 392 | tf_op jit(solution)/shard_map/ppermute | solution.py:21
  244.1 5.8 collective-permute-done.27
  263.7 4.4 collective-permute-done.31
  269.2 11.3 %all-to-all-start = ((f32[64,1,128]{2,1,0:T(1,128)}), f32[64,1,128]{2,1,0:T(1,128)S(1)}, u32[]{:S(2)}, u32[]{:S(2)}) async-start(f32[64,1,128]{2,1,0:T(1,128)} %reshape.136), calls=%async_computation | async-start | bytes 65536 | tf_op jit(solution)/shard_map/all_to_all | solution.py:123
  280.5 9.1 %all-to-all-done = f32[64,1,128]{2,1,0:T(1,128)S(1)} async-done(((f32[64,1,128]{2,1,0:T(1,128)}), f32[64,1,128]{2,1,0:T(1,128)S(1)}, u32[]{:S(2)}, u32[]{:S(2)}) %all-to-all-start) | async-done | bytes 32800 | tf_op jit(solution)/shard_map/all_to_all | solution.py:123
  291.2 4.5 collective-permute-start.32
  297.6 14.0 %all_gather.14 = f32[5,32,512]{2,0,1:T(8,128)S(1)} all-gather(f32[5,4,512]{2,0,1:T(8,128)S(1)} %copy.46), channel_id=1, replica_groups=mesh['grp'=8,'dev'=64] {'grp'}, dimensions={1}, use_global_device_ids=true | all-gather | bytes 368640 | tf_op jit(solution)/shard_map/all_gather | solution.py:116
  322.0 11.1 %all-gather = f32[8,4,512]{2,1,0:T(4,128)S(1)} all-gather(f32[1,4,512]{2,1,0:T(4,128)S(1)} %bitcast.332), channel_id=1, replica_groups=mesh['grp'=8,'dev'=64] {'grp'}, dimensions={0}, use_global_device_ids=true | all-gather | bytes 73728 | tf_op jit(solution)/shard_map/all_gather | solution.py:132
  359.4 4.9 collective-permute-start.42
  366.3 5.8 collective-permute-done.43
  404.0 4.5 collective-permute-done.51
  422.2 4.5 collective-permute-done.55
  440.4 4.6 collective-permute-done.59
  458.7 4.6 collective-permute-done.63
  476.9 4.6 collective-permute-done.67
  495.0 4.6 collective-permute-done.71
  513.2 4.6 collective-permute-done.75
  533.8 4.5 collective-permute-done.79
  551.8 4.5 collective-permute-done.83
  588.3 4.4 collective-permute-done.91
  593.2 16.2 %all_to_all.10 = f32[64,1,128]{2,1,0:T(1,128)S(1)} all-to-all(f32[64,1,128]{2,1,0:T(1,128)S(1)} %reshape.138), channel_id=1, replica_groups=mesh['grp'=8,'dev'=64] {'dev'}, dimensions={0} | all-to-all | bytes 65536 | tf_op jit(solution)/shard_map/all_to_all | solution.py:123
  629.4 11.4 %all-gather.1 = f32[8,4,512]{2,1,0:T(4,128)S(1)} all-gather(f32[1,4,512]{2,1,0:T(4,128)S(1)} %bitcast.331), channel_id=1, replica_groups=mesh['grp'=8,'dev'=64] {'grp'}, dimensions={0}, use_global_device_ids=true | all-gather | bytes 73728 | tf_op jit(solution)/shard_map/all_gather | solution.py:132
  666.5 4.9 collective-permute-start.102
  673.4 5.8 collective-permute-done.103
  711.1 4.5 collective-permute-done.111
  729.2 4.5 collective-permute-done.115
  747.4 4.6 collective-permute-done.119
  765.8 4.6 collective-permute-done.123
  783.9 4.6 collective-permute-done.127
  (545 shorter events, 487.7 us)
Async XLA Ops:
  1.4 12.8 %collective-permute-start.4 = (f32[1,128]{1,0:T(1,128)S(1)}, f32[1,128]{1,0:T(1,128)S(1)}, u32[]{:S(2)}, u32[]{:S(2)}) collective-permute-start(f32[1,128]{1,0:T(1,128)S(1)} %get-tuple-element.105), channel_id=1, source_target_pairs={{0,64},{64,128},{128,192},{192,256},{256,320},{320,384},{384,448},... | collective-permute-start | bytes 1544 | tf_op jit(solution)/shard_map/ppermute | solution.py:21
  5.1 9.0 %collective-permute-start.5 = (f32[1,128]{1,0:T(1,128)S(1)}, f32[1,128]{1,0:T(1,128)S(1)}, u32[]{:S(2)}, u32[]{:S(2)}) collective-permute-start(f32[1,128]{1,0:T(1,128)S(1)} %get-tuple-element.104), channel_id=1, source_target_pairs={{64,0},{128,64},{192,128},{256,192},{320,256},{384,320},{448,384},... | collective-permute-start | bytes 1544 | tf_op jit(solution)/shard_map/ppermute | solution.py:22
  18.0 14.0 %collective-permute-start.2 = (f32[3,66,1]{2,1,0:T(8,128)S(1)}, f32[3,66,1]{2,1,0:T(8,128)S(1)}, u32[]{:S(2)}, u32[]{:S(2)}) collective-permute-start(f32[3,66,1]{2,1,0:T(8,128)S(1)} %get-tuple-element.34), channel_id=1, source_target_pairs={{0,1},{1,2},{2,3},{3,4},{4,5},{5,6},{6,7},{7,8},{8,9},{9,10},{10,1... | collective-permute-start | bytes 2384 | tf_op jit(solution)/shard_map/ppermute | solution.py:21
  21.1 10.9 %collective-permute-start.3 = (f32[3,66,1]{2,1,0:T(8,128)S(1)}, f32[3,66,1]{2,1,0:T(8,128)S(1)}, u32[]{:S(2)}, u32[]{:S(2)}) collective-permute-start(f32[3,66,1]{2,1,0:T(8,128)S(1)} %get-tuple-element.35), channel_id=1, source_target_pairs={{1,0},{2,1},{3,2},{4,3},{5,4},{6,5},{7,6},{8,7},{9,8},{10,9},{11,1... | collective-permute-start | bytes 2384 | tf_op jit(solution)/shard_map/ppermute | solution.py:22
  28.6 8.0 %collective-permute-start.7 = (f32[66,1]{1,0:T(8,128)S(1)}, f32[66,1]{1,0:T(8,128)S(1)}, u32[]{:S(2)}, u32[]{:S(2)}) collective-permute-start(f32[66,1]{1,0:T(8,128)S(1)} %get-tuple-element.59), channel_id=1, source_target_pairs={{0,1},{1,2},{2,3},{3,4},{4,5},{5,6},{6,7},{7,8},{8,9},{9,10},{10,1... | collective-permute-start | bytes 800 | tf_op jit(solution)/shard_map/ppermute | solution.py:21
  48.5 8.0 %collective-permute-start.11 = (f32[66,1]{1,0:T(8,128)S(1)}, f32[66,1]{1,0:T(8,128)S(1)}, u32[]{:S(2)}, u32[]{:S(2)}) collective-permute-start(f32[66,1]{1,0:T(8,128)S(1)} %get-tuple-element.57), channel_id=1, source_target_pairs={{0,1},{1,2},{2,3},{3,4},{4,5},{5,6},{6,7},{7,8},{8,9},{9,10},{10,1... | collective-permute-start | bytes 800 | tf_op jit(solution)/shard_map/ppermute | solution.py:21
  56.7 9.3 %collective-permute-start.12 = (f32[1,128]{1,0:T(1,128)S(1)}, f32[1,128]{1,0:T(1,128)S(1)}, u32[]{:S(2)}, u32[]{:S(2)}) collective-permute-start(f32[1,128]{1,0:T(1,128)S(1)} %get-tuple-element.101), channel_id=1, source_target_pairs={{0,64},{64,128},{128,192},{192,256},{256,320},{320,384},{384,448},... | collective-permute-start | bytes 1544 | tf_op jit(solution)/shard_map/ppermute | solution.py:21
  68.0 8.0 %collective-permute-start.15 = (f32[66,1]{1,0:T(8,128)S(1)}, f32[66,1]{1,0:T(8,128)S(1)}, u32[]{:S(2)}, u32[]{:S(2)}) collective-permute-start(f32[66,1]{1,0:T(8,128)S(1)} %get-tuple-element.55), channel_id=1, source_target_pairs={{0,1},{1,2},{2,3},{3,4},{4,5},{5,6},{6,7},{7,8},{8,9},{9,10},{10,1... | collective-permute-start | bytes 800 | tf_op jit(solution)/shard_map/ppermute | solution.py:21
  90.3 7.8 collective-permute-start.19
  108.2 7.8 collective-permute-start.23
  207.7 27.6 %collective-permute-start.24 = (f32[1,32]{1,0:T(1,128)S(1)}, f32[1,32]{1,0:T(1,128)S(1)}, u32[]{:S(2)}, u32[]{:S(2)}) collective-permute-start(f32[1,32]{1,0:T(1,128)S(1)} %get-tuple-element.169), channel_id=1, source_target_pairs={{0,64},{64,128},{128,192},{192,256},{256,320},{320,384},{384,448},... | collective-permute-start | bytes 392 | tf_op jit(solution)/shard_map/ppermute | solution.py:21
  242.1 7.8 collective-permute-start.27
  269.2 20.5 %all-to-all-start = ((f32[64,1,128]{2,1,0:T(1,128)}), f32[64,1,128]{2,1,0:T(1,128)S(1)}, u32[]{:S(2)}, u32[]{:S(2)}) async-start(f32[64,1,128]{2,1,0:T(1,128)} %reshape.136), calls=%async_computation | async-start | bytes 65536 | tf_op jit(solution)/shard_map/all_to_all | solution.py:123
  291.2 20.5 %collective-permute-start.32 = (f32[1,1024]{1,0:T(1,128)S(1)}, f32[1,1024]{1,0:T(1,128)S(1)}, u32[]{:S(2)}, u32[]{:S(2)}) collective-permute-start(f32[1,1024]{1,0:T(1,128)S(1)} %get-tuple-element.97), channel_id=1, source_target_pairs={{0,64},{64,128},{128,192},{192,256},{256,320},{320,384},{384,448},... | collective-permute-start | bytes 12296 | tf_op jit(solution)/shard_map/ppermute | solution.py:21
  295.7 16.0 %collective-permute-start.33 = (f32[1,1024]{1,0:T(1,128)S(1)}, f32[1,1024]{1,0:T(1,128)S(1)}, u32[]{:S(2)}, u32[]{:S(2)}) collective-permute-start(f32[1,1024]{1,0:T(1,128)S(1)} %get-tuple-element.96), channel_id=1, source_target_pairs={{64,0},{128,64},{192,128},{256,192},{320,256},{384,320},{448,384},... | collective-permute-start | bytes 12296 | tf_op jit(solution)/shard_map/ppermute | solution.py:22
  364.3 7.8 collective-permute-start.43
  400.6 7.8 collective-permute-start.51
  418.8 7.8 collective-permute-start.55
  437.0 8.0 %collective-permute-start.59 = (f32[66,1]{1,0:T(8,128)S(1)}, f32[66,1]{1,0:T(8,128)S(1)}, u32[]{:S(2)}, u32[]{:S(2)}) collective-permute-start(f32[66,1]{1,0:T(8,128)S(1)} %get-tuple-element.53), channel_id=1, source_target_pairs={{0,1},{1,2},{2,3},{3,4},{4,5},{5,6},{6,7},{7,8},{8,9},{9,10},{10,1... | collective-permute-start | bytes 800 | tf_op jit(solution)/shard_map/ppermute | solution.py:21
  455.3 8.0 %collective-permute-start.63 = (f32[66,1]{1,0:T(8,128)S(1)}, f32[66,1]{1,0:T(8,128)S(1)}, u32[]{:S(2)}, u32[]{:S(2)}) collective-permute-start(f32[66,1]{1,0:T(8,128)S(1)} %get-tuple-element.51), channel_id=1, source_target_pairs={{0,1},{1,2},{2,3},{3,4},{4,5},{5,6},{6,7},{7,8},{8,9},{9,10},{10,1... | collective-permute-start | bytes 800 | tf_op jit(solution)/shard_map/ppermute | solution.py:21
  473.5 8.0 %collective-permute-start.67 = (f32[66,1]{1,0:T(8,128)S(1)}, f32[66,1]{1,0:T(8,128)S(1)}, u32[]{:S(2)}, u32[]{:S(2)}) collective-permute-start(f32[66,1]{1,0:T(8,128)S(1)} %get-tuple-element.49), channel_id=1, source_target_pairs={{0,1},{1,2},{2,3},{3,4},{4,5},{5,6},{6,7},{7,8},{8,9},{9,10},{10,1... | collective-permute-start | bytes 800 | tf_op jit(solution)/shard_map/ppermute | solution.py:21
  491.6 8.0 %collective-permute-start.71 = (f32[66,1]{1,0:T(8,128)S(1)}, f32[66,1]{1,0:T(8,128)S(1)}, u32[]{:S(2)}, u32[]{:S(2)}) collective-permute-start(f32[66,1]{1,0:T(8,128)S(1)} %get-tuple-element.47), channel_id=1, source_target_pairs={{0,1},{1,2},{2,3},{3,4},{4,5},{5,6},{6,7},{7,8},{8,9},{9,10},{10,1... | collective-permute-start | bytes 800 | tf_op jit(solution)/shard_map/ppermute | solution.py:21
  509.8 8.0 %collective-permute-start.75 = (f32[66,1]{1,0:T(8,128)S(1)}, f32[66,1]{1,0:T(8,128)S(1)}, u32[]{:S(2)}, u32[]{:S(2)}) collective-permute-start(f32[66,1]{1,0:T(8,128)S(1)} %get-tuple-element.45), channel_id=1, source_target_pairs={{0,1},{1,2},{2,3},{3,4},{4,5},{5,6},{6,7},{7,8},{8,9},{9,10},{10,1... | collective-permute-start | bytes 800 | tf_op jit(solution)/shard_map/ppermute | solution.py:21
  530.4 7.8 collective-permute-start.79
  548.4 7.8 collective-permute-start.83
  585.0 7.8 collective-permute-start.91
  671.4 7.8 collective-permute-start.103
  707.7 7.8 collective-permute-start.111
  725.9 7.8 collective-permute-start.115
  744.1 8.0 %collective-permute-start.119 = (f32[66,1]{1,0:T(8,128)S(1)}, f32[66,1]{1,0:T(8,128)S(1)}, u32[]{:S(2)}, u32[]{:S(2)}) collective-permute-start(f32[66,1]{1,0:T(8,128)S(1)} %get-tuple-element.43), channel_id=1, source_target_pairs={{0,1},{1,2},{2,3},{3,4},{4,5},{5,6},{6,7},{7,8},{8,9},{9,10},{10,1... | collective-permute-start | bytes 800 | tf_op jit(solution)/shard_map/ppermute | solution.py:21
  762.4 8.0 %collective-permute-start.123 = (f32[66,1]{1,0:T(8,128)S(1)}, f32[66,1]{1,0:T(8,128)S(1)}, u32[]{:S(2)}, u32[]{:S(2)}) collective-permute-start(f32[66,1]{1,0:T(8,128)S(1)} %get-tuple-element.41), channel_id=1, source_target_pairs={{0,1},{1,2},{2,3},{3,4},{4,5},{5,6},{6,7},{7,8},{8,9},{9,10},{10,1... | collective-permute-start | bytes 800 | tf_op jit(solution)/shard_map/ppermute | solution.py:21
  780.6 8.0 %collective-permute-start.127 = (f32[66,1]{1,0:T(8,128)S(1)}, f32[66,1]{1,0:T(8,128)S(1)}, u32[]{:S(2)}, u32[]{:S(2)}) collective-permute-start(f32[66,1]{1,0:T(8,128)S(1)} %get-tuple-element.39), channel_id=1, source_target_pairs={{0,1},{1,2},{2,3},{3,4},{4,5},{5,6},{6,7},{7,8},{8,9},{9,10},{10,1... | collective-permute-start | bytes 800 | tf_op jit(solution)/shard_map/ppermute | solution.py:21
  (109 other events, 1101.8 us)
